TPU v7x, 256 devices: a whole 4x4x8 slice. The times are simulated.
256 devices in a mesh: circ: 32 (over z, y), span: 8 (over x, core).
Axes of the slice: x: 4, y: 4, z: 8, core: 2. Of those that a mesh axis runs over, the one named last changes fastest.
Arguments:
- increment: int32 [8], P('span'), may hold values from 1 to 4095, as said below
- partners: int32 [8, 4096], P('span', 'circ'), may hold values from 0 to 4095, as said below
- rotor_faces: float32 [90, 8, 4096], P(None, 'span', 'circ'), as said below
- stator_faces: float32 [90, 8, 4096], P(None, 'span', 'circ'), as said below
- solution: float32 [135, 8, 8192], P(None, 'span', 'circ'), may hold values from -6 to 6
- residual: float32 [135, 8, 8192], P(None, 'span', 'circ'), may hold values from -6 to 6
- inverse_blocks: bfloat16 [135, 135, 8, 8192], P(None, None, 'span', 'circ'), may hold values from -0.25 to 2
- halo_lists: int32 [2, 8, 8192], P(None, 'span', 'circ'), may hold values from 0 to 255, as said below
- lifting: float32 [135, 45], replicated, may hold values from -0.875 to 0.875
- traces: float32 [2, 45, 135], replicated, may hold values from -0.5 to 0.5
- couplings: float32 [2, 135, 45], replicated, may hold values from -0.875 to 0.875
Outputs:
- update: float32 [135, 8, 8192], P(None, 'span', 'circ')
- interface_flux: float32 [45, 8, 4096], P(None, 'span', 'circ')
Inputs may be any that keep to these rules, and one draw needn't show every extreme that they name: No row's increment is a multiple of 128. `partners`: within each span row, the 128 rotor faces of an aligned block name each stator face of the same block exactly once. `halo_lists`: within each aligned block of 256 elements of a row, each list names each position 0 to 255 exactly once. `rotor_faces`: density and pressure are positive at every face point. `stator_faces`: density and pressure are positive at every face point.
All inputs are finite; a program needn't handle non-finite values.
Results may differ from a plain program's by a relative error of at most 0.0003.
Values sent between devices are 32-bit elements; how exact they have to be, the bound alone decides.
A program may use at most 64 MiB of HBM per device.

v0:
```python
import jax
import jax.numpy as jnp
from jax import lax
from jax.sharding import PartitionSpec as P

GAMMA = 1.4
VISCOSITY = 0.3


def shifted(value, axis, steps):
    count = lax.axis_size(axis)
    initial, last = (max(0, -steps), min(count, count - steps))
    return lax.ppermute(value, axis, [(source, source + steps) for source in range(initial, last)])


def euler_flux(state):
    density = state[0]
    mom_x = state[1]
    mom_y = state[2]
    mom_z = state[3]
    energy = state[4]
    vel_x = mom_x / density
    kinetic = 0.5 * (mom_x * mom_x + mom_y * mom_y + mom_z * mom_z) / density
    pressure = (GAMMA - 1.0) * (energy - kinetic)
    flux = jnp.stack(
        [mom_x, mom_x * vel_x + pressure, mom_y * vel_x, mom_z * vel_x, (energy + pressure) * vel_x]
    )
    wave_speed = jnp.abs(vel_x) + jnp.sqrt(GAMMA * pressure / density)
    return (flux, wave_speed)


def mortar(left_side, right_side):
    face_total = left_side.shape[-1]
    left_state = left_side[:45].reshape(5, 9, face_total)
    right_state = right_side[:45].reshape(5, 9, face_total)
    left_flux, left_speed = euler_flux(left_state)
    right_flux, right_speed = euler_flux(right_state)
    fastest = jnp.maximum(left_speed, right_speed)
    common = 0.5 * (left_flux + right_flux) - 0.5 * fastest * (right_state - left_state)
    return common.reshape(45, face_total) - 0.5 * VISCOSITY * (left_side[45:] + right_side[45:])


def shards(
    increment,
    partners,
    rotor_faces,
    stator_faces,
    solution,
    residual,
    inverse_blocks,
    halo_lists,
    lifting,
    traces,
    couplings,
):
    highest = lax.Precision.HIGHEST
    face_count = rotor_faces.shape[2]
    blocks = lax.axis_size("circ")
    my_block = lax.axis_index("circ")
    offset = increment[0]
    whole_steps = offset // face_count % blocks
    remainder = offset % face_count
    rotor_data = rotor_faces[:, 0, :]
    stator_data = stator_faces[:, 0, :]
    slot_iota = jnp.arange(face_count, dtype=jnp.int32)
    wrapped = slot_iota < remainder
    state_now = solution[:, 0, :]
    inverse_now = inverse_blocks[:, :, 0, :]
    residual_now = residual[:, 0, :]
    upper_trace = jnp.dot(traces[0], state_now, precision=highest)
    lower_trace = jnp.dot(traces[1], state_now, precision=highest)
    from_below = shifted(upper_trace, "span", 1)
    from_above = shifted(lower_trace, "span", -1)
    target = (partners[0] + offset) % (blocks * face_count)
    owners = target // face_count
    slot_index = target % face_count
    outgoing = (
        jnp.zeros((blocks, rotor_data.shape[0], face_count), jnp.float32)
        .at[owners, :, slot_index]
        .set(rotor_data.T)
    )
    incoming = lax.all_to_all(outgoing, "circ", split_axis=0, concat_axis=0, tiled=True)
    arrived = jnp.sum(incoming, axis=0)
    mortar_flux = mortar(arrived, stator_data)
    sources = (my_block - whole_steps - wrapped.astype(jnp.int32)) % blocks
    block_iota = jnp.arange(blocks, dtype=jnp.int32)
    replies = jnp.where(block_iota[:, None, None] == sources[None, None, :], mortar_flux[None], 0.0)
    returned = lax.all_to_all(replies, "circ", split_axis=0, concat_axis=0, tiled=True)
    rotor_flux = returned[owners, :, slot_index].T
    face_terms = jnp.concatenate([rotor_flux, -mortar_flux], axis=1)
    lifted = jnp.dot(lifting, face_terms, precision=highest)
    below_nbr = jnp.take(from_below, halo_lists[0, 0], axis=1)
    above_nbr = jnp.take(from_above, halo_lists[1, 0], axis=1)
    coupled = jnp.dot(couplings[0], below_nbr, precision=highest) + jnp.dot(
        couplings[1], above_nbr, precision=highest
    )
    rhs = residual_now - lifted - coupled
    update = jnp.einsum(
        "ije,je->ie", inverse_now, rhs, precision=highest, preferred_element_type=jnp.float32
    )
    return (update[:, None, :], rotor_flux[:, None, :])


def solution(mesh):
    placed = (
        P("span"),
        P("span", "circ"),
        P(None, "span", "circ"),
        P(None, "span", "circ"),
        P(None, "span", "circ"),
        P(None, "span", "circ"),
        P(None, None, "span", "circ"),
        P(None, "span", "circ"),
        P(),
        P(),
        P(),
    )
    return jax.shard_map(
        shards,
        mesh=mesh,
        in_specs=placed,
        out_specs=(P(None, "span", "circ"), P(None, "span", "circ")),
        check_vma=False,
    )
```

profile of v0, /device:TPU:2, one launch (start us, length us, event | category | flops | bytes accessed | tf_op | source)
XLA Modules:
  0.0 102.9 jit_solution(3774804421516963471)
XLA Ops:
  0.6 0.0 copy-start
  1.3 0.9 copy.90
  2.2 0.7 fusion.62
  2.9 0.2 broadcast_in_dim.47
  3.1 6.8 %scatter_fusion = f32[32,90,128]{1,2,0:T(8,128)S(1)} fusion(f32[32,90,128]{1,2,0:T(8,128)S(1)} %broadcast_in_dim.47, s32[128]{0:T(128)S(1)} %fusion.58, f32[128,90]{1,0:T(8,128)S(1)} %bitcast.248), kind=kCustom, calls=%fused_computation.3 | custom fusion | bytes 139264 | tf_op jit(solution)/shard_map/scatter | solution.py:80
  10.0 1.8 %copy.41 = f32[32,90,128]{2,1,0:T(8,128)} copy(f32[32,90,128]{1,2,0:T(8,128)S(1)} %scatter_fusion) | data formatting | bytes 2949120 | tf_op jit(solution)/shard_map/scatter | solution.py:80
  11.8 0.0 copy-start.4
  11.8 0.0 copy-start.1
  11.8 0.0 copy-start.3
  11.8 0.0 copy-start.6
  11.8 11.6 %all-to-all-start = ((f32[32,90,128]{2,1,0:T(8,128)}), f32[32,90,128]{2,1,0:T(8,128)S(1)}, u32[]{:S(2)}, u32[]{:S(2)}) async-start(f32[32,90,128]{2,1,0:T(8,128)} %copy.41), calls=%async_computation | async-start | bytes 3145728 | tf_op jit(solution)/shard_map/all_to_all | solution.py:82
  23.4 0.0 copy-done.4
  23.4 0.1 fusion.66
  23.5 0.0 copy-done.1
  23.5 0.2 fusion.4
  23.7 1.9 %collective-permute-start.1 = (f32[45,256]{1,0:T(8,128)S(1)}, f32[45,256]{1,0:T(8,128)S(1)}, u32[]{:S(2)}, u32[]{:S(2)}) collective-permute-start(f32[45,256]{1,0:T(8,128)S(1)} %fusion.4), channel_id=1, source_target_pairs={{1,0},{2,1},{3,2},{4,3},{5,4},{6,5},{7,6},{9,8},{10,9},{11,10},{12... | collective-permute-start | bytes 138248 | tf_op jit(solution)/shard_map/ppermute | solution.py:13
  25.6 0.2 fusion.6
  25.8 2.4 %collective-permute-start = (f32[45,256]{1,0:T(8,128)S(1)}, f32[45,256]{1,0:T(8,128)S(1)}, u32[]{:S(2)}, u32[]{:S(2)}) collective-permute-start(f32[45,256]{1,0:T(8,128)S(1)} %fusion.6), channel_id=1, source_target_pairs={{0,1},{1,2},{2,3},{3,4},{4,5},{5,6},{6,7},{8,9},{9,10},{10,11},{11... | collective-permute-start | bytes 138248 | tf_op jit(solution)/shard_map/ppermute | solution.py:13
  28.3 0.0 copy-done.3
  28.5 0.0 copy-done.6
  28.6 0.0 copy-start.5
  28.6 33.9 %all-to-all-done = f32[32,90,128]{2,1,0:T(8,128)S(1)} async-done(((f32[32,90,128]{2,1,0:T(8,128)}), f32[32,90,128]{2,1,0:T(8,128)S(1)}, u32[]{:S(2)}, u32[]{:S(2)}) %all-to-all-start) | async-done | bytes 1474592 | tf_op jit(solution)/shard_map/all_to_all | solution.py:82
  62.5 0.1 reduce_sum.9
  62.9 1.0 broadcast_select_fusion
  63.8 5.8 %all-to-all-start.1 = ((f32[32,45,128]{2,1,0:T(8,128)}), f32[32,45,128]{2,1,0:T(8,128)S(1)}, u32[]{:S(2)}, u32[]{:S(2)}) async-start(f32[32,45,128]{2,1,0:T(8,128)} %broadcast_select_fusion), calls=%async_computation.1 | async-start | bytes 1572864 | tf_op jit(solution)/shard_map/all_to_all | solution.py:88
  69.7 0.0 copy-done.5
  69.7 0.1 fusion.65
  69.8 0.0 collective-permute-done.1
  69.8 0.1 copy.66
  69.9 0.7 gather_fusion.2
  70.6 0.0 collective-permute-done
  70.6 0.1 copy.63
  70.7 0.0 copy-start.2
  70.8 0.7 gather_fusion.1
  71.5 0.4 fusion.10
  71.9 19.6 %all-to-all-done.1 = f32[32,45,128]{2,1,0:T(8,128)S(1)} async-done(((f32[32,45,128]{2,1,0:T(8,128)}), f32[32,45,128]{2,1,0:T(8,128)S(1)}, u32[]{:S(2)}, u32[]{:S(2)}) %all-to-all-start.1) | async-done | bytes 737312 | tf_op jit(solution)/shard_map/all_to_all | solution.py:88
  91.5 0.7 copy.60
  92.2 1.2 %gather_fusion = f32[128,45]{1,0:T(8,128)S(1)} fusion(f32[32,45,128]{1,2,0:T(8,128)S(1)} %copy.60, s32[128]{0:T(128)S(1)} %get-tuple-element.9), kind=kCustom, calls=%fused_computation.2 | custom fusion | bytes 47104 | tf_op jit(solution)/shard_map/gather | solution.py:89
  93.4 0.1 copy.61
  93.5 0.0 copy-done
  93.5 0.0 copy-done.2
  93.5 0.4 fusion.3
  93.9 0.4 fusion.2
  94.3 7.1 %multiply_reduce_fusion = f32[256,135]{0,1:T(8,128)S(1)} fusion(f32[256,135]{0,1:T(8,128)S(1)} %fusion.2, bf16[135,135,1,256]{3,1,2,0:T(8,128)(2,1)} %param.19), kind=kLoop, calls=%fused_computation.4 | loop fusion | flops 13962240 | bytes 9607680 | tf_op jit(solution)/shard_map/ije,je->ie/dot_general | solution.py:98
  101.4 0.8 broadcast_in_dim.50
  102.2 0.7 copy.68
  (34 shorter events, 0.3 us)
Async XLA Ops:
  0.6 92.9 %copy-start = (f32[135,45]{0,1:T(8,128)S(1)}, f32[135,45]{0,1:T(8,128)}, u32[]{:S(2)}) copy-start(f32[135,45]{0,1:T(8,128)} %param.21) | copy-start | bytes 72904
  11.8 11.6 %copy-start.4 = (f32[2,45,135]{2,0,1:T(2,128)S(1)}, f32[2,45,135]{2,0,1:T(2,128)}, u32[]{:S(2)}) copy-start(f32[2,45,135]{2,0,1:T(2,128)} %param.22) | copy-start | bytes 145804
  11.8 11.7 %copy-start.1 = (f32[135,1,256]{2,1,0:T(1,128)S(1)}, f32[135,1,256]{2,1,0:T(1,128)}, u32[]{:S(2)}) copy-start(f32[135,1,256]{2,1,0:T(1,128)} %param.17) | copy-start | bytes 414724
  11.8 16.5 %copy-start.3 = (f32[90,1,128]{2,1,0:T(1,128)S(1)}, f32[90,1,128]{2,1,0:T(1,128)}, u32[]{:S(2)}) copy-start(f32[90,1,128]{2,1,0:T(1,128)} %param.16) | copy-start | bytes 138244
  11.8 16.7 %copy-start.6 = (s32[2,1,256]{2,1,0:T(1,128)S(1)}, s32[2,1,256]{2,1,0:T(1,128)}, u32[]{:S(2)}) copy-start(s32[2,1,256]{2,1,0:T(1,128)} %param.20) | copy-start | bytes 6148
  11.8 50.7 %all-to-all-start = ((f32[32,90,128]{2,1,0:T(8,128)}), f32[32,90,128]{2,1,0:T(8,128)S(1)}, u32[]{:S(2)}, u32[]{:S(2)}) async-start(f32[32,90,128]{2,1,0:T(8,128)} %copy.41), calls=%async_computation | async-start | bytes 3145728 | tf_op jit(solution)/shard_map/all_to_all | solution.py:82
  23.7 46.1 %collective-permute-start.1 = (f32[45,256]{1,0:T(8,128)S(1)}, f32[45,256]{1,0:T(8,128)S(1)}, u32[]{:S(2)}, u32[]{:S(2)}) collective-permute-start(f32[45,256]{1,0:T(8,128)S(1)} %fusion.4), channel_id=1, source_target_pairs={{1,0},{2,1},{3,2},{4,3},{5,4},{6,5},{7,6},{9,8},{10,9},{11,10},{12... | collective-permute-start | bytes 138248 | tf_op jit(solution)/shard_map/ppermute | solution.py:13
  25.8 44.8 %collective-permute-start = (f32[45,256]{1,0:T(8,128)S(1)}, f32[45,256]{1,0:T(8,128)S(1)}, u32[]{:S(2)}, u32[]{:S(2)}) collective-permute-start(f32[45,256]{1,0:T(8,128)S(1)} %fusion.6), channel_id=1, source_target_pairs={{0,1},{1,2},{2,3},{3,4},{4,5},{5,6},{6,7},{8,9},{9,10},{10,11},{11... | collective-permute-start | bytes 138248 | tf_op jit(solution)/shard_map/ppermute | solution.py:13
  28.6 41.1 %copy-start.5 = (f32[2,135,45]{1,0,2:T(2,128)S(1)}, f32[2,135,45]{1,0,2:T(2,128)}, u32[]{:S(2)}) copy-start(f32[2,135,45]{1,0,2:T(2,128)} %param.23) | copy-start | bytes 145804
  63.8 27.7 %all-to-all-start.1 = ((f32[32,45,128]{2,1,0:T(8,128)}), f32[32,45,128]{2,1,0:T(8,128)S(1)}, u32[]{:S(2)}, u32[]{:S(2)}) async-start(f32[32,45,128]{2,1,0:T(8,128)} %broadcast_select_fusion), calls=%async_computation.1 | async-start | bytes 1572864 | tf_op jit(solution)/shard_map/all_to_all | solution.py:88
  70.7 22.8 %copy-start.2 = (f32[135,1,256]{2,1,0:T(1,128)S(1)}, f32[135,1,256]{2,1,0:T(1,128)}, u32[]{:S(2)}) copy-start(f32[135,1,256]{2,1,0:T(1,128)} %param.18) | copy-start | bytes 414724
where the time goes:
time: 103 us
  waiting for transfers between devices  53.6 us (52%)
  starting transfers between devices  21.7 us (21%)
  local copies, waits for them, and re-layouts  15.2 us (15%)
  other arithmetic  9 us (9%)
  between operations  1.81 us (2%)
  matrix products  1.54 us (1%)
    all_to_all x1, waiting for transfers between devices, shards(): lax.all_to_all(outgoing, 'circ', split_axis=0, concat_axis=0, tiled=True)  33.9 us
    all_to_all x1, waiting for transfers between devices, shards(): lax.all_to_all(replies, 'circ', split_axis=0, concat_axis=0, tiled=True)  19.6 us
    all_to_all x1, starting transfers between devices, shards(): lax.all_to_all(outgoing, 'circ', split_axis=0, concat_axis=0, tiled=True)  11.6 us
    scatter x2, local copies, waits for them, and re-layouts, shards(): outgoing = jnp.zeros((blocks, rotor_data.shape[0], face_count), jnp.float...  8.65 us
    dot_general x1, other arithmetic, shards(): jnp.einsum('ije,je->ie', inverse_now, rhs, precision=highest, preferred_e...  7.12 us
    all_to_all x1, starting transfers between devices, shards(): lax.all_to_all(replies, 'circ', split_axis=0, concat_axis=0, tiled=True)  5.76 us
    ppermute x2, starting transfers between devices, shifted(): lax.ppermute(value, axis, [(source, source + steps) for source in range(i...  4.33 us
  transfers between devices with their start and end apart: 4, of which 2 were waited for; matrix products, arithmetic and copies ran while one was open for 4% of the time, Pallas kernels for 0%

commit v1 on v0

v1 whole, which is shorter than its diff:
```python
import functools

import jax
import jax.numpy as jnp
from jax import lax
from jax.experimental import pallas as pl
from jax.experimental.pallas import tpu as pltpu
from jax.sharding import PartitionSpec as P

GAMMA = 1.4
VISCOSITY = 0.3
CIRC = 32
SPANS = 8
MESH = pl.DeviceIdType.MESH
NEAR = (1, -1, 2, -2)
MIDDLE = (4, -4)
FAR = (12, -12)
CHUNKS = 5


def two_parts(value):
    head = value.astype(jnp.bfloat16)
    return head, (value - head.astype(jnp.float32)).astype(jnp.bfloat16)


def mxu(left, right, dims=((1,), (0,))):
    return lax.dot_general(left, right, (dims, ((), ())), preferred_element_type=jnp.float32)


def dot3(left, right, dims=((1,), (0,))):
    left_head, left_tail = two_parts(left)
    right_head, right_tail = two_parts(right)
    small = mxu(left_head, right_tail, dims) + mxu(left_tail, right_head, dims)
    return mxu(left_head, right_head, dims) + small


def side_terms(ref):
    var = [ref[9 * v : 9 * v + 9, :] for v in range(5)]
    inverse = 1.0 / var[0]
    vel = var[1] * inverse
    kinetic = 0.5 * (var[1] * var[1] + var[2] * var[2] + var[3] * var[3]) * inverse
    pressure = (GAMMA - 1.0) * (var[4] - kinetic)
    flux = [var[1], var[1] * vel + pressure, var[2] * vel, var[3] * vel, (var[4] + pressure) * vel]
    terms = [
        0.5 * flux[v] - 0.5 * VISCOSITY * ref[45 + 9 * v : 54 + 9 * v, :] for v in range(5)
    ]
    return terms, jnp.abs(vel) + jnp.sqrt(GAMMA * pressure * inverse)


def kernel(
    inc_hbm, partners_hbm, rotor_hbm, stator_hbm, solution_hbm, residual_hbm, inverse_hbm, halo_hbm, lift_hbm,
    traces_hbm, couplings_hbm, update_hbm, flux_hbm,
    inc, partners, rotor, stator, state, residual, inverse, halo, lift, traces, couplings,
    one_hot, sorted_rotor, near_out, near_in, near_rotor, near_stator, middle_out, middle_in, middle_rotor,
    middle_stator, far_out, far_in, last_rotor, last_stator, trace_out, trace_in, lift_parts, lifted_blocks,
    rhs, base, own_terms, own_speed, face_terms, rotor_flux,
    load_sem, block_sem, send_sem, recv_sem, store_sem,
):
    me = lax.axis_index("circ")
    row = lax.axis_index("span")

    def at(circ_shift, span_shift=0):
        return (lax.rem(me + circ_shift + CIRC, CIRC), lax.rem(row + span_shift + SPANS, SPANS))

    barrier = pltpu.get_barrier_semaphore()
    for shift in NEAR + MIDDLE + FAR:
        pl.semaphore_signal(barrier, inc=1, device_id=at(shift), device_id_type=MESH)
    for shift in (1, -1):
        pl.semaphore_signal(barrier, inc=1, device_id=at(0, shift), device_id_type=MESH)

    pairs = [
        (partners_hbm, partners),
        (rotor_hbm.at[:, 0, :], rotor),
        (stator_hbm.at[:, 0, :], stator),
        (traces_hbm.at[:, 0, :], traces.at[0]),
        (traces_hbm.at[:, 1, :], traces.at[1]),
        (solution_hbm.at[:, 0, :], state),
        (lift_hbm, lift),
        (couplings_hbm.at[:, 0, :], couplings.at[0]),
        (couplings_hbm.at[:, 1, :], couplings.at[1]),
        (halo_hbm.at[:, 0, :], halo),
        (residual_hbm.at[:, 0, :], residual),
        (inc_hbm, inc),
    ]
    loads = [pltpu.make_async_copy(src, dst, load_sem.at[k]) for k, (src, dst) in enumerate(pairs)]
    for load in loads:
        load.start()
    rows = 135 // CHUNKS

    def block(k):
        part = pl.ds(rows * k, rows)
        return pltpu.make_async_copy(inverse_hbm.at[part], inverse.at[part], block_sem.at[k])

    for k in range(CHUNKS):
        block(k).start()

    loads[11].wait()
    increment = jnp.broadcast_to(inc[...], (1, 128))
    remainder = jnp.bitwise_and(increment, 127)
    whole = jnp.right_shift(increment, 7)
    lane = lax.broadcasted_iota(jnp.int32, (1, 128), 1)
    steps = whole + jnp.where(lane < remainder, 1, 0)
    digit_near = jnp.bitwise_and(steps + 1, 3) - 1
    quarter = jnp.bitwise_and(jnp.right_shift(steps - digit_near, 2), 7)

    def among(*values):
        hit = quarter == values[0]
        for value in values[1:]:
            hit = jnp.logical_or(hit, quarter == value)
        return jnp.where(hit, 1, 0)

    digit_middle = among(1, 4, 6) - among(2, 7)
    digit_far = among(2, 3, 4) - among(5, 6)

    def copies(first, shifts, sources, landing, span=False):
        made = []
        for k, shift in enumerate(shifts):
            made.append(
                pltpu.make_async_remote_copy(
                    src_ref=sources[k],
                    dst_ref=landing.at[k],
                    send_sem=send_sem.at[first + k],
                    recv_sem=recv_sem.at[first + k],
                    device_id=at(0, shift) if span else at(shift),
                    device_id_type=MESH,
                )
            )
        return made

    def spread(value):
        return jnp.broadcast_to(value, (90, 128))

    loads[0].wait()
    slot = jnp.bitwise_and(partners[...] + remainder, 127)
    sublane = lax.broadcasted_iota(jnp.int32, (128, 128), 0)
    one_hot[...] = jnp.where(sublane == jnp.broadcast_to(slot, (128, 128)), 1.0, 0.0).astype(jnp.bfloat16)
    loads[1].wait()
    faces = rotor[...]
    head, tail = two_parts(faces)
    rest = (faces - head.astype(jnp.float32) - tail.astype(jnp.float32)).astype(jnp.bfloat16)
    turn = one_hot[...]
    across = ((1,), (1,))
    sorted_rotor[...] = mxu(head, turn, across) + (mxu(tail, turn, across) + mxu(rest, turn, across))
    loads[2].wait()

    digit = spread(digit_near)
    near_out[0] = jnp.where(digit == 1, sorted_rotor[...], stator[...])
    near_out[1] = jnp.where(digit == -1, sorted_rotor[...], stator[...])
    near = copies(0, NEAR, [near_out.at[0], near_out.at[1], sorted_rotor, stator], near_in)
    pl.semaphore_wait(barrier, 10)
    for copy in near:
        copy.start()

    for k in range(3, 6):
        loads[k].wait()
    for k in range(2):
        trace_out[k] = dot3(traces[k], state[...])
    spans = copies(8, (1, -1), [trace_out.at[0], trace_out.at[1]], trace_in, span=True)
    for copy in spans:
        copy.start()

    def local_work():
        for k in range(6, 11):
            loads[k].wait()
        head, tail = two_parts(lift[...])
        lift_parts[...] = jnp.zeros((96, 135), jnp.bfloat16)
        lift_parts[0:45, :] = head
        lift_parts[48:93, :] = tail
        factor = lift_parts[...]

        def lift_rows(k, carry):
            block(k).wait()
            for i in range(rows):
                both = mxu(factor, inverse[rows * k + i])
                lifted_blocks[rows * k + i] = both[:48] + both[48:]
            return carry

        lax.fori_loop(0, CHUNKS, lift_rows, 0)
        for copy in spans:
            copy.wait_recv()
        position = lax.broadcasted_iota(jnp.int32, (256, 256), 0)
        total = residual[...]
        for k in range(2):
            edge = 0 if k == 0 else SPANS - 1
            arrived = trace_in[k] * jnp.where(row == edge, 0.0, 1.0)
            wanted = jnp.broadcast_to(halo[pl.ds(k, 1), :], (256, 256))
            pick = jnp.where(position == wanted, 1.0, 0.0).astype(jnp.bfloat16)
            head, tail = two_parts(arrived)
            total = total - dot3(couplings[k], mxu(head, pick) + mxu(tail, pick), ((0,), (0,)))
        rhs[...] = total

        def base_row(i):
            return jnp.sum(inverse[i].astype(jnp.float32) * rhs[...], axis=0, keepdims=True)

        def base_eight(k, carry):
            first = pl.multiple_of(8 * k, 8)
            base[pl.ds(first, 8), :] = jnp.concatenate([base_row(first + i) for i in range(8)], axis=0)
            return carry

        lax.fori_loop(0, 16, base_eight, 0)
        base[128:135, :] = jnp.concatenate([base_row(128 + i) for i in range(7)], axis=0)

    early = me < CIRC // 2

    @pl.when(early)
    def _():
        local_work()

    def merge(digit, plus, minus, rotor_ref, stator_ref, rotor_to, stator_to, two=None):
        digit = spread(digit)
        rotor_new = jnp.where(digit == 0, rotor_ref[...], jnp.where(digit == 1, plus[...], minus[...]))
        stator_new = jnp.where(digit == 0, stator_ref[...], jnp.where(digit == 1, minus[...], plus[...]))
        if two is not None:
            rotor_new = jnp.where(digit == 2, two[0][...], rotor_new)
            stator_new = jnp.where(digit == 2, two[1][...], stator_new)
        rotor_to[...] = rotor_new
        stator_to[...] = stator_new
        return rotor_new, stator_new

    for copy in near:
        copy.wait_recv()
    moved, met = merge(
        digit_near, near_in.at[0], near_in.at[1], sorted_rotor, stator, near_rotor, near_stator,
        (near_in.at[2], near_in.at[3]),
    )
    digit = spread(digit_middle)
    middle_out[0] = jnp.where(digit == 1, moved, met)
    middle_out[1] = jnp.where(digit == -1, moved, met)
    middle = copies(4, MIDDLE, [middle_out.at[0], middle_out.at[1]], middle_in)
    for copy in middle:
        copy.start()

    for copy in middle:
        copy.wait_recv()
    moved, met = merge(
        digit_middle, middle_in.at[0], middle_in.at[1], near_rotor, near_stator, middle_rotor, middle_stator
    )
    digit = spread(digit_far)
    far_out[0] = jnp.where(digit == 1, moved, met)
    far_out[1] = jnp.where(digit == -1, moved, met)
    far = copies(6, FAR, [far_out.at[0], far_out.at[1]], far_in)
    for copy in far:
        copy.start()

    @pl.when(jnp.logical_not(early))
    def _():
        local_work()

    for k, ref in enumerate((sorted_rotor, stator)):
        terms, speed = side_terms(ref)
        for v in range(5):
            own_terms[k, 9 * v : 9 * v + 9, :] = terms[v]
        own_speed[k] = speed

    for copy in far:
        copy.wait_recv()
    merge(digit_far, far_in.at[0], far_in.at[1], middle_rotor, middle_stator, last_rotor, last_stator)

    for k, (left, right) in enumerate(((sorted_rotor, last_stator), (last_rotor, stator))):
        terms, speed = side_terms(last_stator if k == 0 else last_rotor)
        fastest = 0.5 * jnp.maximum(speed, own_speed[k])
        for v in range(5):
            part = pl.ds(9 * v, 9)
            face_terms[k, part, :] = (
                own_terms[k, part, :] + terms[v] - fastest * (right[part, :] - left[part, :])
            )
    head, tail = two_parts(face_terms[0])
    turn = one_hot[...]
    rotor_flux[...] = mxu(head, turn) + mxu(tail, turn)
    store_flux = pltpu.make_async_copy(rotor_flux, flux_hbm.at[:, 0, :], store_sem.at[0])
    store_flux.start()
    terms = jnp.concatenate([-rotor_flux[...], face_terms[1]], axis=1)

    def finish(part):
        weighted = lifted_blocks[part, 0:45, :] * terms[None]
        base[part, :] += jnp.sum(weighted, axis=1)

    def finish_eight(k, carry):
        finish(pl.ds(pl.multiple_of(8 * k, 8), 8))
        return carry

    lax.fori_loop(0, 16, finish_eight, 0)
    finish(pl.ds(128, 7))
    store = pltpu.make_async_copy(base, update_hbm.at[:, 0, :], store_sem.at[1])
    store.start()
    for copy in near + middle + far + spans:
        copy.wait_send()
    store_flux.wait()
    store.wait()


def shards(
    increment,
    partners,
    rotor_faces,
    stator_faces,
    solution,
    residual,
    inverse_blocks,
    halo_lists,
    lifting,
    traces,
    couplings,
):
    def vmem(*shape, dtype=jnp.float32):
        return pltpu.VMEM(shape, dtype)

    face = (90, 128)
    anywhere = pl.BlockSpec(memory_space=pltpu.HBM)
    return pl.pallas_call(
        kernel,
        out_shape=(
            jax.ShapeDtypeStruct((135, 1, 256), jnp.float32),
            jax.ShapeDtypeStruct((45, 1, 128), jnp.float32),
        ),
        in_specs=[anywhere] * 11,
        out_specs=(anywhere, anywhere),
        scratch_shapes=[
            vmem(1, 1, dtype=jnp.int32),
            vmem(1, 128, dtype=jnp.int32),
            vmem(*face),
            vmem(*face),
            vmem(135, 256),
            vmem(135, 256),
            vmem(135, 135, 256, dtype=jnp.bfloat16),
            vmem(2, 256, dtype=jnp.int32),
            vmem(45, 135),
            vmem(2, 45, 135),
            vmem(2, 45, 135),
            vmem(128, 128, dtype=jnp.bfloat16),
            vmem(*face),
            vmem(2, *face),
            vmem(4, *face),
            vmem(*face),
            vmem(*face),
            vmem(2, *face),
            vmem(2, *face),
            vmem(*face),
            vmem(*face),
            vmem(2, *face),
            vmem(2, *face),
            vmem(*face),
            vmem(*face),
            vmem(2, 45, 256),
            vmem(2, 45, 256),
            vmem(96, 135, dtype=jnp.bfloat16),
            vmem(135, 48, 256),
            vmem(135, 256),
            vmem(135, 256),
            vmem(2, 45, 128),
            vmem(2, 9, 128),
            vmem(2, 45, 128),
            vmem(45, 128),
            pltpu.SemaphoreType.DMA((12,)),
            pltpu.SemaphoreType.DMA((CHUNKS,)),
            pltpu.SemaphoreType.DMA((10,)),
            pltpu.SemaphoreType.DMA((10,)),
            pltpu.SemaphoreType.DMA((2,)),
        ],
        compiler_params=pltpu.CompilerParams(
            collective_id=0, has_side_effects=True, vmem_limit_bytes=60 * 1024 * 1024
        ),
    )(
        increment.reshape(1, 1),
        partners,
        rotor_faces,
        stator_faces,
        solution,
        residual,
        inverse_blocks.reshape(135, 135, 256),
        halo_lists,
        lifting.T,
        traces.transpose(1, 0, 2),
        couplings.transpose(2, 0, 1),
    )


def solution(mesh):
    placed = (
        P("span"),
        P("span", "circ"),
        P(None, "span", "circ"),
        P(None, "span", "circ"),
        P(None, "span", "circ"),
        P(None, "span", "circ"),
        P(None, None, "span", "circ"),
        P(None, "span", "circ"),
        P(),
        P(),
        P(),
    )
    return jax.shard_map(
        shards,
        mesh=mesh,
        in_specs=placed,
        out_specs=(P(None, "span", "circ"), P(None, "span", "circ")),
        check_vma=False,
    )
```

time: 103 us -> 29.3 us (0.28)
  the two profiles are of different devices: /device:TPU:2 before, /device:TPU:12 now
where the time goes in v1:
time: 29.3 us; the launch traced here: 29.1 us
  Pallas kernels  24.8 us (85%)
  local copies, waits for them, and re-layouts  3 us (10%)
  between operations  1.29 us (4%)
    pallas_call x1, Pallas kernels, shards(): pl.pallas_call(kernel, out_shape=(jax.ShapeDtypeStruct((135, 1, 256), jnp...  24.8 us
    unnamed x2, local copies, waits for them, and re-layouts  3 us

profile of v1, /device:TPU:12, one launch (start us, length us, event | category | flops | bytes accessed | tf_op | source)
XLA Modules:
  0.0 29.1 jit_solution(9240177380657730136)
XLA Ops:
  1.3 24.8 %shard_map.122 = (f32[135,1,256]{2,1,0:T(1,128)}, f32[45,1,128]{2,1,0:T(1,128)}) custom-call(s32[1,1]{1,0:T(1,128)} %bitcast.5.inc_hbm, s32[1,128]{1,0:T(1,128)} %partners_hbm.1, f32[90,1,128]{2,1,0:T(1,128)} %rotor_hbm.1, f32[90,1,128]{2,1,0:T(1,128)} %stator_hbm.1, f32[135,1,256]{2,1,0:T(1,128)} %solution_hbm.1, f32[135,1,256]{2,1,0:T(1,128)} %residual_hbm.1, ...), custom_call_target="tpu_custom_call" | custom-call | tf_op jit(solution)/shard_map/pallas_call | solution.py:310
  26.1 1.7 %copy.16 = f32[135,1,256]{2,1,0:T(1,128)} copy(f32[135,1,256]{2,1,0:T(1,128)} %get-tuple-element.4) | data formatting | bytes 276480
  27.8 1.3 %copy.17 = f32[45,1,128]{2,1,0:T(1,128)} copy(f32[45,1,128]{2,1,0:T(1,128)} %get-tuple-element.5) | data formatting | bytes 46080

commit v2 on v1

v2 whole, which is shorter than its diff:
```python
import functools

import jax
import jax.numpy as jnp
from jax import lax
from jax.experimental import pallas as pl
from jax.experimental.pallas import tpu as pltpu
from jax.sharding import PartitionSpec as P

GAMMA = 1.4
VISCOSITY = 0.3
CIRC = 32
SPANS = 8
MESH = pl.DeviceIdType.MESH
STEPS = {"near": (1, -1, 2, -2), "middle": (4, -4), "far": (12, -12)}
KINDS = ("near", "middle", "far")
ORDERS = (("far", "middle", "near"), ("near", "middle", "far"))
STAY = 4
DIGITS = 6
PER_STAGE = 7
CHUNKS = 5
KA = 50 * 1024 * 1024
KB = 4 * 1024 * 1024


def two_parts(value):
    head = value.astype(jnp.bfloat16)
    return head, (value - head.astype(jnp.float32)).astype(jnp.bfloat16)


def mxu(left, right, dims=((1,), (0,))):
    return lax.dot_general(left, right, (dims, ((), ())), preferred_element_type=jnp.float32)


def dot3(left, right, dims=((1,), (0,))):
    left_head, left_tail = two_parts(left)
    right_head, right_tail = two_parts(right)
    small = mxu(left_head, right_tail, dims) + mxu(left_tail, right_head, dims)
    return mxu(left_head, right_head, dims) + small


def side_terms(ref):
    var = [ref[9 * v : 9 * v + 9, :] for v in range(5)]
    inverse = 1.0 / var[0]
    vel = var[1] * inverse
    kinetic = 0.5 * (var[1] * var[1] + var[2] * var[2] + var[3] * var[3]) * inverse
    pressure = (GAMMA - 1.0) * (var[4] - kinetic)
    flux = [var[1], var[1] * vel + pressure, var[2] * vel, var[3] * vel, (var[4] + pressure) * vel]
    terms = [
        0.5 * flux[v] - 0.5 * VISCOSITY * ref[45 + 9 * v : 54 + 9 * v, :] for v in range(5)
    ]
    return terms, jnp.abs(vel) + jnp.sqrt(GAMMA * pressure * inverse)


def kernel(
    inc_hbm, partners_hbm, rotor_hbm, stator_hbm, solution_hbm, residual_hbm, inverse_hbm, halo_hbm, lift_hbm,
    traces_hbm, couplings_hbm, lifted_blocks, base, terms_ref, rotor_flux,
    inc, partners, rotor, stator, state, residual, inverse, halo, lift, traces, couplings,
    one_hot, sorted_rotor, own_digits, guest_digits, moving, last_rotor, last_stator,
    slots_out, slots_in, trace_out, trace_in, lift_parts, rhs, own_terms, own_speed, face_terms,
    load_sem, block_sem, send_sem, recv_sem,
):
    me = lax.axis_index("circ")
    row = lax.axis_index("span")

    def at(circ_shift, span_shift=0):
        return (lax.rem(me + circ_shift + CIRC, CIRC), lax.rem(row + span_shift + SPANS, SPANS))

    even = lax.rem(row, 2) == 0
    odd = jnp.logical_not(even)
    first_even, last_even = STEPS[ORDERS[0][0]], STEPS[ORDERS[0][2]]
    every = STEPS["far"] + STEPS["middle"] + STEPS["near"]
    barrier = pltpu.get_barrier_semaphore()

    def greet(circ_shift, span_shift):
        pl.semaphore_signal(barrier, inc=1, device_id=at(circ_shift, span_shift), device_id_type=MESH)

    @pl.when(even)
    def _():
        for shift in last_even:
            greet(shift, 1)
        greet(0, 1)
        greet(0, -1)

    @pl.when(odd)
    def _():
        for shift in every:
            greet(shift, 0)
        for shift in first_even:
            greet(shift, -1)
        greet(0, -1)
        greet(0, 1)

    pairs = [
        (partners_hbm, partners),
        (inc_hbm, inc),
        (rotor_hbm.at[:, 0, :], rotor),
        (stator_hbm.at[:, 0, :], stator),
        (traces_hbm.at[:, 0, :], traces.at[0]),
        (traces_hbm.at[:, 1, :], traces.at[1]),
        (solution_hbm.at[:, 0, :], state),
        (lift_hbm, lift),
        (couplings_hbm.at[:, 0, :], couplings.at[0]),
        (couplings_hbm.at[:, 1, :], couplings.at[1]),
        (halo_hbm.at[:, 0, :], halo),
        (residual_hbm.at[:, 0, :], residual),
    ]
    loads = [pltpu.make_async_copy(src, dst, load_sem.at[k]) for k, (src, dst) in enumerate(pairs)]
    for load in loads[:4]:
        load.start()
    rows = 135 // CHUNKS

    def block(k):
        part = pl.ds(rows * k, rows)
        return pltpu.make_async_copy(inverse_hbm.at[part], inverse.at[part], block_sem.at[k])

    def load_rest():
        for load in loads[4:]:
            load.start()
        for k in range(CHUNKS):
            block(k).start()

    early = me < CIRC // 2
    late = jnp.logical_not(early)

    @pl.when(early)
    def _():
        load_rest()

    loads[0].wait()
    loads[1].wait()
    increment = jnp.broadcast_to(inc[...], (1, 128))
    remainder = jnp.bitwise_and(increment, 127)
    whole = jnp.right_shift(increment, 7)
    lane = lax.broadcasted_iota(jnp.int32, (1, 128), 1)
    steps = whole + jnp.where(lane < remainder, 1, 0)
    near_digit = jnp.bitwise_and(steps + 1, 3) - 1
    quarter = jnp.bitwise_and(jnp.right_shift(steps - near_digit, 2), 7)

    def among(*values):
        hit = quarter == values[0]
        for value in values[1:]:
            hit = jnp.logical_or(hit, quarter == value)
        return jnp.where(hit, 1, 0)

    middle_digit = among(1, 4, 6) - among(2, 7)
    far_digit = among(2, 3, 4) - among(5, 6)

    own_digits[...] = jnp.zeros((8, 128), jnp.float32)
    for k, value in enumerate((near_digit, middle_digit, far_digit)):
        own_digits[k : k + 1, :] = value.astype(jnp.float32)

    def slot_copy(group, stage, k, device, source):
        index = (3 * group + stage) * PER_STAGE + k
        return pltpu.make_async_remote_copy(
            src_ref=source,
            dst_ref=guest_digits if k == DIGITS else slots_in.at[6 * (3 * group + stage) + k],
            send_sem=send_sem.at[index],
            recv_sem=recv_sem.at[index],
            device_id=device,
            device_id_type=MESH,
        )

    def stage_copies(group, stage, rotor_ref, stator_ref):
        change = 0 if group == 1 or stage == 1 else 1 if stage == 0 else -1
        out = 2 * (3 * group + stage)
        sources = [slots_out.at[out], slots_out.at[out + 1], rotor_ref, stator_ref]
        made = [
            slot_copy(group, stage, k, at(shift, change), sources[k])
            for k, shift in enumerate(STEPS[ORDERS[group][stage]])
        ]
        if change:
            made.append(slot_copy(group, stage, STAY, at(0, change), rotor_ref))
            made.append(slot_copy(group, stage, STAY + 1, at(0, change), stator_ref))
        if change == 1:
            made.append(slot_copy(group, stage, DIGITS, at(0, change), own_digits))
        return made

    def digit_of(group, stage, digits):
        kind = KINDS.index(ORDERS[group][stage])
        return jnp.broadcast_to(digits[kind : kind + 1, :], (90, 128))

    def prepare(group, stage, digits, rotor_now, stator_now):
        digit = digit_of(group, stage, digits)
        out = 2 * (3 * group + stage)
        slots_out[out] = jnp.where(digit == 1.0, rotor_now, stator_now)
        slots_out[out + 1] = jnp.where(digit == -1.0, rotor_now, stator_now)

    def start(copies):
        for copy in copies:
            copy.start()

    def land(group, stage, copies, digits, rotor_ref, stator_ref, rotor_to, stator_to):
        for copy in copies:
            copy.wait_recv()
        digit = digit_of(group, stage, digits)
        slot = 6 * (3 * group + stage)
        plus, minus = slots_in[slot], slots_in[slot + 1]
        if group == 0 and stage != 1:
            rotor_ref, stator_ref = slots_in.at[slot + STAY], slots_in.at[slot + STAY + 1]
        rotor_new = jnp.where(digit == 0.0, rotor_ref[...], jnp.where(digit == 1.0, plus, minus))
        stator_new = jnp.where(digit == 0.0, stator_ref[...], jnp.where(digit == 1.0, minus, plus))
        if ORDERS[group][stage] == "near":
            rotor_new = jnp.where(digit == 2.0, slots_in[slot + 2], rotor_new)
            stator_new = jnp.where(digit == 2.0, slots_in[slot + 3], stator_new)
        rotor_to[...] = rotor_new
        stator_to[...] = stator_new
        return rotor_new, stator_new

    slot = jnp.bitwise_and(partners[...] + remainder, 127)
    sublane = lax.broadcasted_iota(jnp.int32, (128, 128), 0)
    one_hot[...] = jnp.where(sublane == jnp.broadcast_to(slot, (128, 128)), 1.0, 0.0).astype(jnp.bfloat16)
    turn = one_hot[...]
    across = ((1,), (1,))
    loads[2].wait()
    faces = rotor[...]
    head, tail = two_parts(faces)
    rest = (faces - head.astype(jnp.float32) - tail.astype(jnp.float32)).astype(jnp.bfloat16)
    in_order = mxu(head, turn, across) + (mxu(tail, turn, across) + mxu(rest, turn, across))
    sorted_rotor[...] = in_order
    loads[3].wait()
    for group, mine in enumerate((even, odd)):

        @pl.when(mine)
        def _(group=group):
            prepare(group, 0, own_digits, sorted_rotor[...], stator[...])

    spans = [
        pltpu.make_async_remote_copy(
            src_ref=trace_out.at[k],
            dst_ref=trace_in.at[k],
            send_sem=send_sem.at[6 * PER_STAGE + k],
            recv_sem=recv_sem.at[6 * PER_STAGE + k],
            device_id=at(0, shift),
            device_id_type=MESH,
        )
        for k, shift in enumerate((1, -1))
    ]

    def make_traces():
        for k in range(4, 7):
            loads[k].wait()
        for k in range(2):
            trace_out[k] = dot3(traces[k], state[...])

    def lift_blocks():
        loads[7].wait()
        head, tail = two_parts(lift[...])
        lift_parts[...] = jnp.zeros((96, 135), jnp.bfloat16)
        lift_parts[0:45, :] = head
        lift_parts[48:93, :] = tail
        factor = lift_parts[...]

        def lift_rows(k, carry):
            block(k).wait()
            for i in range(rows):
                both = mxu(factor, inverse[rows * k + i])
                lifted_blocks[rows * k + i] = both[:48] + both[48:]
            return carry

        lax.fori_loop(0, CHUNKS, lift_rows, 0)

    def multiply_base():
        for k in range(8, 12):
            loads[k].wait()
        for copy in spans:
            copy.wait_recv()
        position = lax.broadcasted_iota(jnp.int32, (256, 256), 0)
        total = residual[...]
        for k in range(2):
            edge = 0 if k == 0 else SPANS - 1
            arrived = trace_in[k] * jnp.where(row == edge, 0.0, 1.0)
            wanted = jnp.broadcast_to(halo[pl.ds(k, 1), :], (256, 256))
            pick = jnp.where(position == wanted, 1.0, 0.0).astype(jnp.bfloat16)
            head, tail = two_parts(arrived)
            total = total - dot3(couplings[k], mxu(head, pick) + mxu(tail, pick), ((0,), (0,)))
        rhs[...] = total

        def base_row(i):
            return jnp.sum(inverse[i].astype(jnp.float32) * rhs[...], axis=0, keepdims=True)

        def base_eight(k, carry):
            first = pl.multiple_of(8 * k, 8)
            base[pl.ds(first, 8), :] = jnp.concatenate([base_row(first + i) for i in range(8)], axis=0)
            return carry

        lax.fori_loop(0, 16, base_eight, 0)
        base[128:135, :] = jnp.concatenate([base_row(128 + i) for i in range(7)], axis=0)

    @pl.when(early)
    def _():
        make_traces()
        lift_blocks()

    @pl.when(even)
    def _():
        pl.semaphore_wait(barrier, len(first_even) + 2)
        start(stage_copies(0, 0, sorted_rotor, stator))

    @pl.when(odd)
    def _():
        pl.semaphore_wait(barrier, len(every) + len(last_even) + 2)
        start(stage_copies(1, 0, sorted_rotor, stator))

    @pl.when(late)
    def _():
        load_rest()
        make_traces()

    for copy in spans:
        copy.start()

    @pl.when(odd)
    def _():
        for stage in (1, 2):
            for group in (0, 1):
                digits = guest_digits if group == 0 else own_digits
                before = stage_copies(group, stage - 1, sorted_rotor, stator)
                if stage == 1:
                    rotor_ref, stator_ref = sorted_rotor, stator
                else:
                    rotor_ref, stator_ref = moving.at[2 * group], moving.at[2 * group + 1]
                to = 2 * group + (4 if stage == 2 else 0)
                moved, met = land(
                    group, stage - 1, before, digits, rotor_ref, stator_ref, moving.at[to], moving.at[to + 1]
                )
                prepare(group, stage, digits, moved, met)
                start(stage_copies(group, stage, moving.at[to], moving.at[to + 1]))

    @pl.when(late)
    def _():
        lift_blocks()

    multiply_base()

    for k, ref in enumerate((sorted_rotor, stator)):
        terms, speed = side_terms(ref)
        for v in range(5):
            own_terms[k, pl.ds(9 * v, 9), :] = terms[v]
        own_speed[k] = speed

    for group, mine in enumerate((even, odd)):

        @pl.when(mine)
        def _(group=group):
            arriving = stage_copies(group, 2, moving.at[6], moving.at[7])
            land(group, 2, arriving, own_digits, moving.at[6], moving.at[7], last_rotor, last_stator)

    for k, (left, right) in enumerate(((sorted_rotor, last_stator), (last_rotor, stator))):
        terms, speed = side_terms(last_stator if k == 0 else last_rotor)
        fastest = 0.5 * jnp.maximum(speed, own_speed[k])
        for v in range(5):
            part = pl.ds(9 * v, 9)
            face_terms[k, part, :] = (
                own_terms[k, part, :] + terms[v] - fastest * (right[part, :] - left[part, :])
            )
    head, tail = two_parts(face_terms[0])
    turn = one_hot[...]
    flux = mxu(head, turn) + mxu(tail, turn)
    rotor_flux[...] = flux
    terms_ref[:, 0:128] = -flux
    terms_ref[:, 128:256] = face_terms[1]
    for copy in spans:
        copy.wait_send()

    @pl.when(even)
    def _():
        for copy in stage_copies(0, 0, sorted_rotor, stator):
            copy.wait_send()

    @pl.when(odd)
    def _():
        for group, stage in ((1, 0), (0, 1), (1, 1), (0, 2), (1, 2)):
            to = 2 * group + (4 if stage == 2 else 0)
            for copy in stage_copies(group, stage, moving.at[to], moving.at[to + 1]):
                copy.wait_send()


def finish_kernel(lifted_blocks, base, terms_ref, rotor_flux, update_hbm, flux_hbm, update, store_sem):
    store_flux = pltpu.make_async_copy(rotor_flux, flux_hbm.at[:, 0, :], store_sem.at[0])
    store_flux.start()
    terms = terms_ref[...]

    def finish(part):
        weighted = lifted_blocks[part, 0:45, :] * terms[None]
        update[part, :] = base[part, :] + jnp.sum(weighted, axis=1)

    def finish_eight(k, carry):
        finish(pl.ds(pl.multiple_of(8 * k, 8), 8))
        return carry

    stores = []
    for k, (start, stop) in enumerate(((0, 64), (64, 128), (128, 135))):
        if stop == 135:
            finish(pl.ds(start, 7))
        else:
            lax.fori_loop(start // 8, stop // 8, finish_eight, 0)
        part = pl.ds(start, stop - start)
        store = pltpu.make_async_copy(update.at[part], update_hbm.at[part, 0, :], store_sem.at[1 + k])
        store.start()
        stores.append(store)
    store_flux.wait()
    for store in stores:
        store.wait()


def shards(
    increment,
    partners,
    rotor_faces,
    stator_faces,
    solution,
    residual,
    inverse_blocks,
    halo_lists,
    lifting,
    traces,
    couplings,
):
    def vmem(*shape, dtype=jnp.float32):
        return pltpu.VMEM(shape, dtype)

    face = (90, 128)
    anywhere = pl.BlockSpec(memory_space=pltpu.HBM)
    held = pl.pallas_call(
        kernel,
        out_shape=(
            vmem(135, 48, 256),
            vmem(135, 256),
            vmem(45, 256),
            vmem(45, 128),
        ),
        in_specs=[anywhere] * 11,
        out_specs=[pl.BlockSpec(memory_space=pltpu.VMEM)] * 4,
        scratch_shapes=[
            vmem(1, 1, dtype=jnp.int32),
            vmem(1, 128, dtype=jnp.int32),
            vmem(*face),
            vmem(*face),
            vmem(135, 256),
            vmem(135, 256),
            vmem(135, 135, 256, dtype=jnp.bfloat16),
            vmem(2, 256, dtype=jnp.int32),
            vmem(45, 135),
            vmem(2, 45, 135),
            vmem(2, 45, 135),
            vmem(128, 128, dtype=jnp.bfloat16),
            vmem(*face),
            vmem(8, 128),
            vmem(8, 128),
            vmem(8, *face),
            vmem(*face),
            vmem(*face),
            vmem(12, *face),
            vmem(36, *face),
            vmem(2, 45, 256),
            vmem(2, 45, 256),
            vmem(96, 135, dtype=jnp.bfloat16),
            vmem(135, 256),
            vmem(2, 45, 128),
            vmem(2, 9, 128),
            vmem(2, 45, 128),
            pltpu.SemaphoreType.DMA((12,)),
            pltpu.SemaphoreType.DMA((CHUNKS,)),
            pltpu.SemaphoreType.DMA((6 * PER_STAGE + 2,)),
            pltpu.SemaphoreType.DMA((6 * PER_STAGE + 2,)),
        ],
        compiler_params=pltpu.CompilerParams(
            collective_id=0, has_side_effects=True, vmem_limit_bytes=KA
        ),
    )(
        increment.reshape(1, 1),
        partners,
        rotor_faces,
        stator_faces,
        solution,
        residual,
        inverse_blocks.reshape(135, 135, 256),
        halo_lists,
        lifting.T,
        traces.transpose(1, 0, 2),
        couplings.transpose(2, 0, 1),
    )
    return pl.pallas_call(
        finish_kernel,
        out_shape=(
            jax.ShapeDtypeStruct((135, 1, 256), jnp.float32),
            jax.ShapeDtypeStruct((45, 1, 128), jnp.float32),
        ),
        in_specs=[pl.BlockSpec(memory_space=pltpu.VMEM)] * 4,
        out_specs=(anywhere, anywhere),
        scratch_shapes=[vmem(135, 256), pltpu.SemaphoreType.DMA((4,))],
        compiler_params=pltpu.CompilerParams(vmem_limit_bytes=KB),
    )(*held)


def solution(mesh):
    placed = (
        P("span"),
        P("span", "circ"),
        P(None, "span", "circ"),
        P(None, "span", "circ"),
        P(None, "span", "circ"),
        P(None, "span", "circ"),
        P(None, None, "span", "circ"),
        P(None, "span", "circ"),
        P(),
        P(),
        P(),
    )
    return jax.shard_map(
        shards,
        mesh=mesh,
        in_specs=placed,
        out_specs=(P(None, "span", "circ"), P(None, "span", "circ")),
        check_vma=False,
    )
```

time: 29.3 us -> 25.4 us (0.87)
  the two profiles are of different devices: /device:TPU:12 before, /device:TPU:2 now
where the time goes in v2:
time: 25.4 us; the launch traced here: 25.2 us
  Pallas kernels  24 us (94%)
  between operations  1.29 us (5%)
    pallas_call x1, Pallas kernels, shards(): pl.pallas_call(kernel, out_shape=(vmem(135, 48, 256), vmem(135, 256), vme...  22.5 us
    pallas_call x1, Pallas kernels, shards(): pl.pallas_call(finish_kernel, out_shape=(jax.ShapeDtypeStruct((135, 1, 25...  1.49 us

profile of v2, /device:TPU:2, one launch (start us, length us, event | category | flops | bytes accessed | tf_op | source)
XLA Modules:
  0.0 25.2 jit_solution(13469736948566998089)
XLA Ops:
  1.3 22.5 %shard_map.122 = (f32[135,48,256]{2,1,0:T(8,128)S(1)}, f32[135,256]{1,0:T(8,128)S(1)}, f32[45,256]{1,0:T(8,128)S(1)}, f32[45,128]{1,0:T(8,128)S(1)}) custom-call(s32[1,1]{1,0:T(1,128)} %bitcast.5.inc_hbm, s32[1,128]{1,0:T(1,128)} %partners_hbm.1, f32[90,1,128]{2,1,0:T(1,128)} %rotor_hbm.1, f32[90,1,128]{2,1,0:T(1,128)} %stator_hbm.1, ...), custom_call_target="tpu_custom_call" | custom-call | tf_op jit(solution)/shard_map/pallas_call | solution.py:425
  23.7 1.5 %shard_map.123 = (f32[135,1,256]{2,1,0:T(1,128)}, f32[45,1,128]{2,1,0:T(1,128)}) custom-call(f32[135,48,256]{2,1,0:T(8,128)S(1)} %get-tuple-element.6.lifted_blocks, f32[135,256]{1,0:T(8,128)S(1)} %get-tuple-element.7.base, f32[45,256]{1,0:T(8,128)S(1)} %get-tuple-element.8.terms_ref, f32[45,128]{1,0:T(8,128)S(1)} %get-tuple-element.9.rotor_flux), custom_call_target="tpu_custom_call" | custom-call | tf_op jit(solution)/shard_map/pallas_call | solution.py:484

commit v3 on v2

--- a/solution.py
+++ b/solution.py
@@ -14,7 +14,7 @@
 MESH = pl.DeviceIdType.MESH
 STEPS = {"near": (1, -1, 2, -2), "middle": (4, -4), "far": (12, -12)}
 KINDS = ("near", "middle", "far")
-ORDERS = (("far", "middle", "near"), ("near", "middle", "far"))
+ORDERS = (("middle", "far", "near"), ("near", "middle", "far"))
 STAY = 4
 DIGITS = 6
 PER_STAGE = 7
@@ -65,31 +65,6 @@
 
     def at(circ_shift, span_shift=0):
         return (lax.rem(me + circ_shift + CIRC, CIRC), lax.rem(row + span_shift + SPANS, SPANS))
-
-    even = lax.rem(row, 2) == 0
-    odd = jnp.logical_not(even)
-    first_even, last_even = STEPS[ORDERS[0][0]], STEPS[ORDERS[0][2]]
-    every = STEPS["far"] + STEPS["middle"] + STEPS["near"]
-    barrier = pltpu.get_barrier_semaphore()
-
-    def greet(circ_shift, span_shift):
-        pl.semaphore_signal(barrier, inc=1, device_id=at(circ_shift, span_shift), device_id_type=MESH)
-
-    @pl.when(even)
-    def _():
-        for shift in last_even:
-            greet(shift, 1)
-        greet(0, 1)
-        greet(0, -1)
-
-    @pl.when(odd)
-    def _():
-        for shift in every:
-            greet(shift, 0)
-        for shift in first_even:
-            greet(shift, -1)
-        greet(0, -1)
-        greet(0, 1)
 
     pairs = [
         (partners_hbm, partners),
@@ -108,6 +83,31 @@
     loads = [pltpu.make_async_copy(src, dst, load_sem.at[k]) for k, (src, dst) in enumerate(pairs)]
     for load in loads[:4]:
         load.start()
+    even = lax.rem(row, 2) == 0
+    odd = jnp.logical_not(even)
+    first_even, last_even = STEPS[ORDERS[0][0]], STEPS[ORDERS[0][2]]
+    every = STEPS["far"] + STEPS["middle"] + STEPS["near"]
+    barrier = pltpu.get_barrier_semaphore()
+
+    def greet(circ_shift, span_shift):
+        pl.semaphore_signal(barrier, inc=1, device_id=at(circ_shift, span_shift), device_id_type=MESH)
+
+    @pl.when(even)
+    def _():
+        for shift in last_even:
+            greet(shift, 1)
+        greet(0, 1)
+        greet(0, -1)
+
+    @pl.when(odd)
+    def _():
+        for shift in first_even:
+            greet(shift, -1)
+        for shift in every:
+            greet(shift, 0)
+        greet(0, -1)
+        greet(0, 1)
+
     rows = 135 // CHUNKS
 
     def block(k):
@@ -120,7 +120,7 @@
         for k in range(CHUNKS):
             block(k).start()
 
-    early = me < CIRC // 2
+    early = me < 12
     late = jnp.logical_not(early)
 
     @pl.when(early)
@@ -260,7 +260,7 @@
 
         lax.fori_loop(0, CHUNKS, lift_rows, 0)
 
-    def multiply_base():
+    def make_rhs():
         for k in range(8, 12):
             loads[k].wait()
         for copy in spans:
@@ -276,6 +276,7 @@
             total = total - dot3(couplings[k], mxu(head, pick) + mxu(tail, pick), ((0,), (0,)))
         rhs[...] = total
 
+    def multiply_base():
         def base_row(i):
             return jnp.sum(inverse[i].astype(jnp.float32) * rhs[...], axis=0, keepdims=True)
 
@@ -313,6 +314,8 @@
     @pl.when(odd)
     def _():
         for stage in (1, 2):
+            if stage == 2:
+                make_rhs()
             for group in (0, 1):
                 digits = guest_digits if group == 0 else own_digits
                 before = stage_copies(group, stage - 1, sorted_rotor, stator)
@@ -331,6 +334,10 @@
     def _():
         lift_blocks()
 
+    @pl.when(even)
+    def _():
+        make_rhs()
+
     multiply_base()
 
     for k, ref in enumerate((sorted_rotor, stator)):
@@ -338,6 +345,21 @@
         for v in range(5):
             own_terms[k, pl.ds(9 * v, 9), :] = terms[v]
         own_speed[k] = speed
+
+    for copy in spans:
+        copy.wait_send()
+
+    @pl.when(even)
+    def _():
+        for copy in stage_copies(0, 0, sorted_rotor, stator):
+            copy.wait_send()
+
+    @pl.when(odd)
+    def _():
+        for group, stage in ((1, 0), (0, 1), (1, 1), (0, 2), (1, 2)):
+            to = 2 * group + (4 if stage == 2 else 0)
+            for copy in stage_copies(group, stage, moving.at[to], moving.at[to + 1]):
+                copy.wait_send()
 
     for group, mine in enumerate((even, odd)):
 
@@ -360,20 +382,6 @@
     rotor_flux[...] = flux
     terms_ref[:, 0:128] = -flux
     terms_ref[:, 128:256] = face_terms[1]
-    for copy in spans:
-        copy.wait_send()
-
-    @pl.when(even)
-    def _():
-        for copy in stage_copies(0, 0, sorted_rotor, stator):
-            copy.wait_send()
-
-    @pl.when(odd)
-    def _():
-        for group, stage in ((1, 0), (0, 1), (1, 1), (0, 2), (1, 2)):
-            to = 2 * group + (4 if stage == 2 else 0)
-            for copy in stage_copies(group, stage, moving.at[to], moving.at[to + 1]):
-                copy.wait_send()
 
 
 def finish_kernel(lifted_blocks, base, terms_ref, rotor_flux, update_hbm, flux_hbm, update, store_sem):

time: 25.4 us -> 23.9 us (0.941)
  the two profiles are of different devices: /device:TPU:2 before, /device:TPU:25 now
where the time goes in v3:
time: 23.9 us; the launch traced here: 23.7 us
  Pallas kernels  22.5 us (94%)
  between operations  1.29 us (5%)
    pallas_call x1, Pallas kernels, shards(): pl.pallas_call(kernel, out_shape=(vmem(135, 48, 256), vmem(135, 256), vme...  21 us
    pallas_call x1, Pallas kernels, shards(): pl.pallas_call(finish_kernel, out_shape=(jax.ShapeDtypeStruct((135, 1, 25...  1.49 us

profile of v3, /device:TPU:25, one launch (start us, length us, event | category | flops | bytes accessed | tf_op | source)
XLA Modules:
  0.0 23.7 jit_solution(413913652239153431)
XLA Ops:
  1.3 21.0 %shard_map.122 = (f32[135,48,256]{2,1,0:T(8,128)S(1)}, f32[135,256]{1,0:T(8,128)S(1)}, f32[45,256]{1,0:T(8,128)S(1)}, f32[45,128]{1,0:T(8,128)S(1)}) custom-call(s32[1,1]{1,0:T(1,128)} %bitcast.5.inc_hbm, s32[1,128]{1,0:T(1,128)} %partners_hbm.1, f32[90,1,128]{2,1,0:T(1,128)} %rotor_hbm.1, f32[90,1,128]{2,1,0:T(1,128)} %stator_hbm.1, ...), custom_call_target="tpu_custom_call" | custom-call | tf_op jit(solution)/shard_map/pallas_call | solution.py:433
  22.2 1.5 %shard_map.123 = (f32[135,1,256]{2,1,0:T(1,128)}, f32[45,1,128]{2,1,0:T(1,128)}) custom-call(f32[135,48,256]{2,1,0:T(8,128)S(1)} %get-tuple-element.6.lifted_blocks, f32[135,256]{1,0:T(8,128)S(1)} %get-tuple-element.7.base, f32[45,256]{1,0:T(8,128)S(1)} %get-tuple-element.8.terms_ref, f32[45,128]{1,0:T(8,128)S(1)} %get-tuple-element.9.rotor_flux), custom_call_target="tpu_custom_call" | custom-call | tf_op jit(solution)/shard_map/pallas_call | solution.py:492

commit v4 on v3

--- a/solution.py
+++ b/solution.py
@@ -41,15 +41,14 @@
 
 def side_terms(ref):
     var = [ref[9 * v : 9 * v + 9, :] for v in range(5)]
-    inverse = 1.0 / var[0]
-    vel = var[1] * inverse
-    kinetic = 0.5 * (var[1] * var[1] + var[2] * var[2] + var[3] * var[3]) * inverse
+    vel = var[1] / var[0]
+    kinetic = 0.5 * (var[1] * var[1] + var[2] * var[2] + var[3] * var[3]) / var[0]
     pressure = (GAMMA - 1.0) * (var[4] - kinetic)
     flux = [var[1], var[1] * vel + pressure, var[2] * vel, var[3] * vel, (var[4] + pressure) * vel]
     terms = [
         0.5 * flux[v] - 0.5 * VISCOSITY * ref[45 + 9 * v : 54 + 9 * v, :] for v in range(5)
     ]
-    return terms, jnp.abs(vel) + jnp.sqrt(GAMMA * pressure * inverse)
+    return terms, jnp.abs(vel) + jnp.sqrt(GAMMA * pressure / var[0])
 
 
 def kernel(
@@ -65,6 +64,31 @@
 
     def at(circ_shift, span_shift=0):
         return (lax.rem(me + circ_shift + CIRC, CIRC), lax.rem(row + span_shift + SPANS, SPANS))
+
+    even = lax.rem(row, 2) == 0
+    odd = jnp.logical_not(even)
+    first_even, last_even = STEPS[ORDERS[0][0]], STEPS[ORDERS[0][2]]
+    every = STEPS["far"] + STEPS["middle"] + STEPS["near"]
+    barrier = pltpu.get_barrier_semaphore()
+
+    def greet(circ_shift, span_shift):
+        pl.semaphore_signal(barrier, inc=1, device_id=at(circ_shift, span_shift), device_id_type=MESH)
+
+    @pl.when(even)
+    def _():
+        for shift in last_even:
+            greet(shift, 1)
+        greet(0, 1)
+        greet(0, -1)
+
+    @pl.when(odd)
+    def _():
+        for shift in first_even:
+            greet(shift, -1)
+        for shift in every:
+            greet(shift, 0)
+        greet(0, -1)
+        greet(0, 1)
 
     pairs = [
         (partners_hbm, partners),
@@ -83,31 +107,6 @@
     loads = [pltpu.make_async_copy(src, dst, load_sem.at[k]) for k, (src, dst) in enumerate(pairs)]
     for load in loads[:4]:
         load.start()
-    even = lax.rem(row, 2) == 0
-    odd = jnp.logical_not(even)
-    first_even, last_even = STEPS[ORDERS[0][0]], STEPS[ORDERS[0][2]]
-    every = STEPS["far"] + STEPS["middle"] + STEPS["near"]
-    barrier = pltpu.get_barrier_semaphore()
-
-    def greet(circ_shift, span_shift):
-        pl.semaphore_signal(barrier, inc=1, device_id=at(circ_shift, span_shift), device_id_type=MESH)
-
-    @pl.when(even)
-    def _():
-        for shift in last_even:
-            greet(shift, 1)
-        greet(0, 1)
-        greet(0, -1)
-
-    @pl.when(odd)
-    def _():
-        for shift in first_even:
-            greet(shift, -1)
-        for shift in every:
-            greet(shift, 0)
-        greet(0, -1)
-        greet(0, 1)
-
     rows = 135 // CHUNKS
 
     def block(k):
@@ -120,7 +119,7 @@
         for k in range(CHUNKS):
             block(k).start()
 
-    early = me < 12
+    early = me < 11
     late = jnp.logical_not(early)
 
     @pl.when(early)
@@ -380,29 +379,46 @@
     turn = one_hot[...]
     flux = mxu(head, turn) + mxu(tail, turn)
     rotor_flux[...] = flux
-    terms_ref[:, 0:128] = -flux
-    terms_ref[:, 128:256] = face_terms[1]
+    terms_ref[45:48, :] = jnp.zeros((3, 256), jnp.float32)
+    terms_ref[0:45, 0:128] = -flux
+    terms_ref[0:45, 128:256] = face_terms[1]
 
 
 def finish_kernel(lifted_blocks, base, terms_ref, rotor_flux, update_hbm, flux_hbm, update, store_sem):
     store_flux = pltpu.make_async_copy(rotor_flux, flux_hbm.at[:, 0, :], store_sem.at[0])
     store_flux.start()
-    terms = terms_ref[...]
+    terms = [terms_ref[8 * t : 8 * t + 8, :] for t in range(6)]
+    sublane = lax.broadcasted_iota(jnp.int32, (8, 256), 0)
+    lower = [jnp.bitwise_and(sublane, step) == 0 for step in (1, 2, 4)]
+
+    def sum_sublanes(arrays):
+        for k, mask in enumerate(lower):
+            arrays = [
+                jnp.where(mask, first, second) + pltpu.roll(jnp.where(mask, second, first), 1 << k, 0)
+                for first, second in zip(arrays[0::2], arrays[1::2])
+            ]
+        return arrays[0]
+
+    def row_tile(i):
+        parts = [lifted_blocks[i, 8 * t : 8 * t + 8, :] * terms[t] for t in range(6)]
+        return ((parts[0] + parts[1]) + (parts[2] + parts[3])) + (parts[4] + parts[5])
+
+    def finish_eight(k, carry):
+        first = pl.multiple_of(8 * k, 8)
+        part = pl.ds(first, 8)
+        update[part, :] = base[part, :] + sum_sublanes([row_tile(first + i) for i in range(8)])
+        return carry
 
     def finish(part):
-        weighted = lifted_blocks[part, 0:45, :] * terms[None]
-        update[part, :] = base[part, :] + jnp.sum(weighted, axis=1)
-
-    def finish_eight(k, carry):
-        finish(pl.ds(pl.multiple_of(8 * k, 8), 8))
-        return carry
+        rest = [row_tile(128 + i) for i in range(7)]
+        update[part, :] = base[part, :] + sum_sublanes(rest + rest[:1])[0:7]
 
     stores = []
     for k, (start, stop) in enumerate(((0, 64), (64, 128), (128, 135))):
         if stop == 135:
             finish(pl.ds(start, 7))
         else:
-            lax.fori_loop(start // 8, stop // 8, finish_eight, 0)
+            lax.fori_loop(start // 8, stop // 8, finish_eight, 0, unroll=4)
         part = pl.ds(start, stop - start)
         store = pltpu.make_async_copy(update.at[part], update_hbm.at[part, 0, :], store_sem.at[1 + k])
         store.start()
@@ -435,7 +451,7 @@
         out_shape=(
             vmem(135, 48, 256),
             vmem(135, 256),
-            vmem(45, 256),
+            vmem(48, 256),
             vmem(45, 128),
         ),
         in_specs=[anywhere] * 11,

time: 23.9 us -> 23.3 us (0.975)
  the two profiles are of different devices: /device:TPU:25 before, /device:TPU:2 now
where the time goes in v4:
time: 23.3 us; the launch traced here: 23 us
  Pallas kernels  21.7 us (93%)
  between operations  1.29 us (6%)
    pallas_call x1, Pallas kernels, shards(): pl.pallas_call(kernel, out_shape=(vmem(135, 48, 256), vmem(135, 256), vme...  20.5 us
    pallas_call x1, Pallas kernels, shards(): pl.pallas_call(finish_kernel, out_shape=(jax.ShapeDtypeStruct((135, 1, 25...  1.2 us

profile of v4, /device:TPU:2, one launch (start us, length us, event | category | flops | bytes accessed | tf_op | source)
XLA Modules:
  0.0 23.0 jit_solution(16097319167682671340)
XLA Ops:
  1.3 20.5 %shard_map.122 = (f32[135,48,256]{2,1,0:T(8,128)S(1)}, f32[135,256]{1,0:T(8,128)S(1)}, f32[48,256]{1,0:T(8,128)S(1)}, f32[45,128]{1,0:T(8,128)S(1)}) custom-call(s32[1,1]{1,0:T(1,128)} %bitcast.5.inc_hbm, s32[1,128]{1,0:T(1,128)} %partners_hbm.1, f32[90,1,128]{2,1,0:T(1,128)} %rotor_hbm.1, f32[90,1,128]{2,1,0:T(1,128)} %stator_hbm.1, ...), custom_call_target="tpu_custom_call" | custom-call | tf_op jit(solution)/shard_map/pallas_call | solution.py:449
  21.8 1.2 %shard_map.123 = (f32[135,1,256]{2,1,0:T(1,128)}, f32[45,1,128]{2,1,0:T(1,128)}) custom-call(f32[135,48,256]{2,1,0:T(8,128)S(1)} %get-tuple-element.6.lifted_blocks, f32[135,256]{1,0:T(8,128)S(1)} %get-tuple-element.7.base, f32[48,256]{1,0:T(8,128)S(1)} %get-tuple-element.8.terms_ref, f32[45,128]{1,0:T(8,128)S(1)} %get-tuple-element.9.rotor_flux), custom_call_target="tpu_custom_call" | custom-call | tf_op jit(solution)/shard_map/pallas_call | solution.py:508

commit v5 on v4

--- a/solution.py
+++ b/solution.py
@@ -119,7 +119,7 @@
         for k in range(CHUNKS):
             block(k).start()
 
-    early = me < 11
+    early = me < 10
     late = jnp.logical_not(early)
 
     @pl.when(early)
@@ -418,7 +418,7 @@
         if stop == 135:
             finish(pl.ds(start, 7))
         else:
-            lax.fori_loop(start // 8, stop // 8, finish_eight, 0, unroll=4)
+            lax.fori_loop(start // 8, stop // 8, finish_eight, 0, unroll=8)
         part = pl.ds(start, stop - start)
         store = pltpu.make_async_copy(update.at[part], update_hbm.at[part, 0, :], store_sem.at[1 + k])
         store.start()

time: 23.3 us -> 23.3 us (level)
  no operation moved by 1% of the time
where the time goes in v5:
time: 23.3 us; the launch traced here: 23 us
  Pallas kernels  21.7 us (93%)
  between operations  1.29 us (6%)
    pallas_call x1, Pallas kernels, shards(): pl.pallas_call(kernel, out_shape=(vmem(135, 48, 256), vmem(135, 256), vme...  20.5 us
    pallas_call x1, Pallas kernels, shards(): pl.pallas_call(finish_kernel, out_shape=(jax.ShapeDtypeStruct((135, 1, 25...  1.19 us

profile of v5, /device:TPU:2, one launch (start us, length us, event | category | flops | bytes accessed | tf_op | source)
XLA Modules:
  0.0 23.0 jit_solution(9574178844176763955)
XLA Ops:
  1.3 20.5 %shard_map.122 = (f32[135,48,256]{2,1,0:T(8,128)S(1)}, f32[135,256]{1,0:T(8,128)S(1)}, f32[48,256]{1,0:T(8,128)S(1)}, f32[45,128]{1,0:T(8,128)S(1)}) custom-call(s32[1,1]{1,0:T(1,128)} %bitcast.5.inc_hbm, s32[1,128]{1,0:T(1,128)} %partners_hbm.1, f32[90,1,128]{2,1,0:T(1,128)} %rotor_hbm.1, f32[90,1,128]{2,1,0:T(1,128)} %stator_hbm.1, ...), custom_call_target="tpu_custom_call" | custom-call | tf_op jit(solution)/shard_map/pallas_call | solution.py:449
  21.8 1.2 %shard_map.123 = (f32[135,1,256]{2,1,0:T(1,128)}, f32[45,1,128]{2,1,0:T(1,128)}) custom-call(f32[135,48,256]{2,1,0:T(8,128)S(1)} %get-tuple-element.6.lifted_blocks, f32[135,256]{1,0:T(8,128)S(1)} %get-tuple-element.7.base, f32[48,256]{1,0:T(8,128)S(1)} %get-tuple-element.8.terms_ref, f32[45,128]{1,0:T(8,128)S(1)} %get-tuple-element.9.rotor_flux), custom_call_target="tpu_custom_call" | custom-call | tf_op jit(solution)/shard_map/pallas_call | solution.py:508
